TPU v7x, 256 devices: a whole 4x4x8 slice. The times are simulated.
256 devices in a mesh: row: 32 (over y, z_hi, core), col: 8 (over z_lo, x).
Axes of the slice: x: 4, y: 4, z: 8 (z_hi: 4, z_lo: 2; z = z_hi * 2 + z_lo), core: 2. Of those that a mesh axis runs over, the one named last changes fastest.
Arguments:
- tokens: bfloat16 [1024, 8192], P('row', 'col'), may hold values from -6 to 6
- w_gate: bfloat16 [28672, 8192], P('row', 'col'), may hold values from -0.0625 to 0.0625
- w_up: bfloat16 [28672, 8192], P('row', 'col'), may hold values from -0.0625 to 0.0625
- w_down: bfloat16 [28672, 8192], P('row', 'col'), may hold values from -0.03125 to 0.03125
- grad_out: bfloat16 [1024, 8192], P('row', 'col'), may hold values from -6 to 6
Outputs:
- grad_in: bfloat16 [1024, 8192], P('row', 'col')
- grad_gate: bfloat16 [28672, 8192], P('row', 'col')
- grad_up: bfloat16 [28672, 8192], P('row', 'col')
- grad_down: bfloat16 [28672, 8192], P('row', 'col')
All inputs are finite; a program needn't handle non-finite values.
Results may differ from a plain program's by a relative error of at most 0.03.
Values may be sent and summed in bfloat16 or wider, within the bound.
A program may use at most 128 MiB of HBM per device.

v0:
```python
import jax
import jax.numpy as jnp
from jax import lax
from jax.sharding import PartitionSpec as P


def col_partial(operand, weight):
    product = lax.dot_general(
        operand, weight, (((1,), (1,)), ((), ())), preferred_element_type=jnp.float32
    )
    return lax.optimization_barrier(product.astype(jnp.bfloat16)).astype(jnp.float32)


def weight_grad(grads, inputs):
    return lax.dot_general(
        grads, inputs, (((0,), (0,)), ((), ())), preferred_element_type=jnp.float32
    )


def pointwise(gate_pre, up_pre, hid_grad):
    logistic = 1.0 / (1.0 + jnp.exp(-gate_pre))
    activated = gate_pre * logistic
    hidden = (activated * up_pre).astype(jnp.bfloat16)
    up_grad = (hid_grad * activated).astype(jnp.bfloat16)
    gate_grad = (hid_grad * up_pre * logistic * (1.0 + gate_pre * (1.0 - logistic))).astype(
        jnp.bfloat16
    )
    return (hidden, gate_grad, up_grad)


def local(tokens, w_gate, w_up, w_down, grad_out):
    tok_full, out_full = (
        lax.all_gather(tokens, "row", axis=0, tiled=True),
        lax.all_gather(grad_out, "row", axis=0, tiled=True),
    )
    token_count = tok_full.shape[0]
    loss_scale = float(token_count) ** (-0.5)
    partials = (
        col_partial(tok_full, w_gate),
        col_partial(tok_full, w_up),
        col_partial(out_full, w_down),
    )
    gate_pre, up_pre, hid_grad = (
        lax.psum_scatter(
            partials[0].astype(jnp.bfloat16), "col", scatter_dimension=0, tiled=True
        ).astype(jnp.float32),
        lax.psum_scatter(
            partials[1].astype(jnp.bfloat16), "col", scatter_dimension=0, tiled=True
        ).astype(jnp.float32),
        lax.psum_scatter(
            partials[2].astype(jnp.bfloat16), "col", scatter_dimension=0, tiled=True
        ).astype(jnp.float32),
    )
    hidden, gate_grad, up_grad = pointwise(gate_pre, up_pre, hid_grad)
    hidden_piece = lax.all_gather(hidden, "col", axis=0, tiled=True)
    gate_piece = lax.all_gather(gate_grad, "col", axis=0, tiled=True)
    up_piece = lax.all_gather(up_grad, "col", axis=0, tiled=True)
    input_rows = jnp.dot(gate_piece, w_gate, preferred_element_type=jnp.float32) + jnp.dot(
        up_piece, w_up, preferred_element_type=jnp.float32
    )
    acc_gate = weight_grad(gate_piece, tok_full)
    acc_up = weight_grad(up_piece, tok_full)
    acc_down = weight_grad(hidden_piece, out_full)
    grad_in = lax.psum_scatter(
        input_rows.astype(jnp.bfloat16), "row", scatter_dimension=0, tiled=True
    )
    return (
        grad_in,
        (acc_gate * loss_scale).astype(jnp.bfloat16),
        (acc_up * loss_scale).astype(jnp.bfloat16),
        (acc_down * loss_scale).astype(jnp.bfloat16),
    )


def solution(mesh):
    in_specs = (P("row", "col"), P("row", "col"), P("row", "col"), P("row", "col"), P("row", "col"))
    out_specs = (P("row", "col"), P("row", "col"), P("row", "col"), P("row", "col"))
    return jax.shard_map(local, mesh=mesh, in_specs=in_specs, out_specs=out_specs, check_vma=False)
```

profile of v0, /device:TPU:1, one launch (start us, length us, event | category | flops | bytes accessed | tf_op | source)
XLA Modules:
  0.0 494.9 jit_solution(11601401887328840655)
XLA Ops:
  7.2 0.7 all-gather.6.cloned.1.call-update
  8.0 0.7 all-gather.8.cloned.1.call-update
  8.7 60.9 %all-gather.6.cloned.1.call-done = bf16[1024,1024]{1,0:T(8,128)(2,1)} async-done(((bf16[32,1024]{1,0:T(8,128)(2,1)}), bf16[1024,1024]{1,0:T(8,128)(2,1)}) %all-gather.6.cloned.1.call-update) | async-done | bytes 2097168 | tf_op jit(solution)/shard_map/all_gather | solution.py:34
  69.6 5.7 %convolution_convert_fusion.2 = bf16[1024,896]{1,0:T(8,128)(2,1)} fusion(bf16[1024,1024]{1,0:T(8,128)(2,1)} %all-gather.6.cloned.1.call-done, bf16[896,1024]{1,0:T(8,128)(2,1)} %param.8), kind=kOutput, calls=%fused_computation.6 | convolution fusion | flops 1879965696 | bytes 5767168 | tf_op jit(solution)/shard_map/dot_general | solution.py:8
  75.4 0.0 reduce-scatter.9.cloned.1.call-start
  75.4 48.5 %all-gather.8.cloned.1.call-done = bf16[1024,1024]{1,0:T(8,128)(2,1)} async-done(((bf16[32,1024]{1,0:T(8,128)(2,1)}), bf16[1024,1024]{1,0:T(8,128)(2,1)}) %all-gather.8.cloned.1.call-update) | async-done | bytes 2097168 | tf_op jit(solution)/shard_map/all_gather | solution.py:33
  123.9 5.2 %convolution_convert_fusion = bf16[1024,896]{1,0:T(8,128)(2,1)} fusion(bf16[1024,1024]{1,0:T(8,128)(2,1)} %all-gather.8.cloned.1.call-done, bf16[896,1024]{1,0:T(8,128)(2,1)S(1)} %copy-done), kind=kOutput, calls=%fused_computation.4 | convolution fusion | flops 1879965696 | bytes 5767168 | tf_op jit(solution)/shard_map/dot_general | solution.py:8
  129.2 5.7 %convolution_convert_fusion.1 = bf16[1024,896]{1,0:T(8,128)(2,1)} fusion(bf16[1024,1024]{1,0:T(8,128)(2,1)} %all-gather.8.cloned.1.call-done, bf16[896,1024]{1,0:T(8,128)(2,1)} %param.7), kind=kOutput, calls=%fused_computation.5 | convolution fusion | flops 1879965696 | bytes 5767168 | tf_op jit(solution)/shard_map/dot_general | solution.py:8
  135.0 27.5 %reduce-scatter.5.cloned.1.call-done = bf16[128,896]{1,0:T(8,128)(2,1)} async-done(((bf16[1024,896]{1,0:T(8,128)(2,1)}), bf16[128,896]{1,0:T(8,128)(2,1)}) %reduce-scatter.5.cloned.1.call-update) | async-done | bytes 229392 | tf_op jit(solution)/shard_map/reduce_scatter | solution.py:50
  162.5 46.5 %reduce-scatter.9.cloned.1.call-done = bf16[128,896]{1,0:T(8,128)(2,1)} async-done(((bf16[1024,896]{1,0:T(8,128)(2,1)}), bf16[128,896]{1,0:T(8,128)(2,1)}) %reduce-scatter.9.cloned.1.call-update) | async-done | bytes 229392 | tf_op jit(solution)/shard_map/reduce_scatter | solution.py:44
  209.1 46.0 %reduce-scatter.7.cloned.1.call-done = bf16[128,896]{1,0:T(8,128)(2,1)} async-done(((bf16[1024,896]{1,0:T(8,128)(2,1)}), bf16[128,896]{1,0:T(8,128)(2,1)}) %reduce-scatter.7.cloned.1.call-update) | async-done | bytes 229392 | tf_op jit(solution)/shard_map/reduce_scatter | solution.py:47
  255.0 2.2 fusion.4
  257.4 0.7 all-gather.12.cloned.1.call-update
  258.1 0.7 all-gather.14.cloned.1.call-update
  258.8 0.2 reduce-scatter.11.cloned.1.call-start
  259.0 40.6 %all-gather.10.cloned.1.call-done = bf16[1024,896]{1,0:T(8,128)(2,1)} async-done(((bf16[128,896]{1,0:T(8,128)(2,1)}), bf16[1024,896]{1,0:T(8,128)(2,1)}) %all-gather.10.cloned.1.call-update) | async-done | bytes 1835024 | tf_op jit(solution)/shard_map/all_gather | solution.py:56
  299.6 5.8 %fusion.9 = f32[1024,1024]{1,0:T(8,128)} fusion(bf16[1024,896]{1,0:T(8,128)(2,1)} %all-gather.10.cloned.1.call-done, bf16[896,1024]{1,0:T(8,128)(2,1)S(1)} %copy-done), kind=kOutput, calls=%fused_computation.22 | convolution fusion | flops 1879048192 | bytes 7864320 | tf_op jit(solution)/shard_map/dot_general | solution.py:58
  305.4 39.3 %all-gather.12.cloned.1.call-done = bf16[1024,896]{1,0:T(8,128)(2,1)} async-done(((bf16[128,896]{1,0:T(8,128)(2,1)}), bf16[1024,896]{1,0:T(8,128)(2,1)}) %all-gather.12.cloned.1.call-update) | async-done | bytes 1835024 | tf_op jit(solution)/shard_map/all_gather | solution.py:57
  344.7 7.0 %add_convert_fusion = bf16[1024,1024]{1,0:T(8,128)(2,1)} fusion(f32[1024,1024]{1,0:T(8,128)} %fusion.9, bf16[1024,896]{1,0:T(8,128)(2,1)} %all-gather.12.cloned.1.call-done, bf16[896,1024]{1,0:T(8,128)(2,1)} %param.7), kind=kOutput, calls=%fused_computation | convolution fusion | flops 1881145344 | bytes 9961472 | tf_op jit(solution)/shard_map/dot_general | solution.py:58
  351.8 5.6 %multiply_convert_fusion.1 = bf16[896,1024]{1,0:T(8,128)(2,1)} fusion(bf16[1024,896]{1,0:T(8,128)(2,1)} %all-gather.12.cloned.1.call-done, bf16[1024,1024]{1,0:T(8,128)(2,1)} %all-gather.8.cloned.1.call-done), kind=kOutput, calls=%fused_computation.2 | convolution fusion | flops 1880883200 | bytes 5767168 | tf_op jit(solution)/shard_map/dot_general | solution.py:15
  357.4 3.4 multiply_convert_fusion.2
  360.8 29.0 %all-gather.14.cloned.1.call-done = bf16[1024,896]{1,0:T(8,128)(2,1)} async-done(((bf16[128,896]{1,0:T(8,128)(2,1)}), bf16[1024,896]{1,0:T(8,128)(2,1)}) %all-gather.14.cloned.1.call-update) | async-done | bytes 1835024 | tf_op jit(solution)/shard_map/all_gather | solution.py:55
  389.7 5.5 %multiply_convert_fusion = bf16[896,1024]{1,0:T(8,128)(2,1)} fusion(bf16[1024,896]{1,0:T(8,128)(2,1)} %all-gather.14.cloned.1.call-done, bf16[1024,1024]{1,0:T(8,128)(2,1)} %all-gather.6.cloned.1.call-done), kind=kOutput, calls=%fused_computation.1 | convolution fusion | flops 1880883200 | bytes 5767168 | tf_op jit(solution)/shard_map/dot_general | solution.py:15
  395.2 93.2 %reduce-scatter.11.cloned.1.call-done = bf16[32,1024]{1,0:T(8,128)(2,1)} async-done(((bf16[1024,1024]{1,0:T(8,128)(2,1)}), bf16[32,1024]{1,0:T(8,128)(2,1)}) %reduce-scatter.11.cloned.1.call-update) | async-done | bytes 65552 | tf_op jit(solution)/shard_map/reduce_scatter | solution.py:64
  (18 shorter events, 0.4 us)
Async XLA Ops:
  7.2 116.7 %copy-start = (bf16[896,1024]{1,0:T(8,128)(2,1)S(1)}, bf16[896,1024]{1,0:T(8,128)(2,1)}, u32[]{:S(2)}) copy-start(bf16[896,1024]{1,0:T(8,128)(2,1)} %param.6) | copy-start | bytes 5505028
  7.2 62.4 %all-gather.6.cloned.1.call-start = ((), (), s32[]{:S(2)}) async-start(), calls=%async_computation.4 | async-start | bytes 2162688 | tf_op jit(solution)/shard_map/all_gather | solution.py:34
  7.9 116.0 %all-gather.8.cloned.1.call-start = ((), (), s32[]{:S(2)}) async-start(), calls=%async_computation.6 | async-start | bytes 2162688 | tf_op jit(solution)/shard_map/all_gather | solution.py:33
  8.7 153.9 %reduce-scatter.5.cloned.1.call-start = ((), (), s32[]{:S(2)}) async-start(), calls=%async_computation.5 | async-start | bytes 2064384 | tf_op jit(solution)/shard_map/reduce_scatter | solution.py:50
  75.4 133.7 %reduce-scatter.9.cloned.1.call-start = ((), (), s32[]{:S(2)}) async-start(), calls=%async_computation.8 | async-start | bytes 2064384 | tf_op jit(solution)/shard_map/reduce_scatter | solution.py:44
  129.1 125.9 %reduce-scatter.7.cloned.1.call-start = ((), (), s32[]{:S(2)}) async-start(), calls=%async_computation.7 | async-start | bytes 2064384 | tf_op jit(solution)/shard_map/reduce_scatter | solution.py:47
  134.9 164.7 %all-gather.10.cloned.1.call-start = ((), (), s32[]{:S(2)}) async-start(), calls=%async_computation.9 | async-start | bytes 2064384 | tf_op jit(solution)/shard_map/all_gather | solution.py:56
  257.3 87.4 %all-gather.12.cloned.1.call-start = ((), (), s32[]{:S(2)}) async-start(), calls=%async_computation.10 | async-start | bytes 2064384 | tf_op jit(solution)/shard_map/all_gather | solution.py:57
  258.1 131.7 %all-gather.14.cloned.1.call-start = ((), (), s32[]{:S(2)}) async-start(), calls=%async_computation.12 | async-start | bytes 2064384 | tf_op jit(solution)/shard_map/all_gather | solution.py:55
  258.8 229.6 %reduce-scatter.11.cloned.1.call-start = ((), (), s32[]{:S(2)}) async-start(), calls=%async_computation.11 | async-start | bytes 2162688 | tf_op jit(solution)/shard_map/reduce_scatter | solution.py:64
  351.7 5.6 %copy-start.1 = (bf16[1024,1024]{1,0:T(8,128)(2,1)S(1)}, bf16[1024,1024]{1,0:T(8,128)(2,1)}, u32[]{:S(2)}) copy-start(bf16[1024,1024]{1,0:T(8,128)(2,1)} %all-gather.8.cloned.1.call-done) | copy-start | bytes 6291460
  351.8 5.6 %copy-start.2 = (bf16[1024,896]{1,0:T(8,128)(2,1)S(1)}, bf16[1024,896]{1,0:T(8,128)(2,1)}, u32[]{:S(2)}) copy-start(bf16[1024,896]{1,0:T(8,128)(2,1)} %all-gather.10.cloned.1.call-done) | copy-start | bytes 5505028
Sparse Core Ops, SparseCore 0:
  10.6 58.9 all-gather.5
  72.2 51.7 all-gather.7
  127.1 35.4 reduce-scatter.4
  165.5 43.4 reduce-scatter.8
  212.1 42.9 reduce-scatter.6
  257.4 42.1 all-gather.9
  302.0 42.6 all-gather.11
  347.1 42.6 all-gather.13
  394.2 94.1 reduce-scatter.10
where the time goes:
time: 496 us; the launch traced here: 495 us
  waiting for transfers between devices  434 us (88%)
  matrix products  43.9 us (9%)
  between operations  13.9 us (3%)
    reduce_scatter x1, waiting for transfers between devices, local(): lax.psum_scatter(input_rows.astype(jnp.bfloat16), 'row', scatter_dimensio...  93.2 us
    all_gather x1, waiting for transfers between devices, local(): lax.all_gather(grad_out, 'row', axis=0, tiled=True)  60.9 us
    all_gather x1, waiting for transfers between devices, local(): lax.all_gather(tokens, 'row', axis=0, tiled=True)  48.5 us
    reduce_scatter x1, waiting for transfers between devices, local(): lax.psum_scatter(partials[0].astype(jnp.bfloat16), 'col', scatter_dimensi...  46.5 us
    reduce_scatter x1, waiting for transfers between devices, local(): lax.psum_scatter(partials[1].astype(jnp.bfloat16), 'col', scatter_dimensi...  46 us
    all_gather x1, waiting for transfers between devices, local(): gate_piece = lax.all_gather(gate_grad, 'col', axis=0, tiled=True)  40.6 us
    all_gather x1, waiting for transfers between devices, local(): up_piece = lax.all_gather(up_grad, 'col', axis=0, tiled=True)  39.3 us
    all_gather x1, waiting for transfers between devices, local(): hidden_piece = lax.all_gather(hidden, 'col', axis=0, tiled=True)  29 us
  transfers between devices with their start and end apart: 9, of which 9 were waited for; matrix products, arithmetic and copies ran while one was open for 9% of the time, Pallas kernels for 0%

commit v1 on v0

v1 whole, which is shorter than its diff:
```python
import jax
import jax.numpy as jnp
from jax import lax
from jax.experimental import pallas as pl
from jax.experimental.pallas import tpu as pltpu
from jax.sharding import PartitionSpec as P

NY, NZ, NX = 4, 4, 4
F32, BF16 = jnp.float32, jnp.bfloat16


def mm(a, b, dims):
    return lax.dot_general(a, b, (dims, ((), ())), preferred_element_type=F32)


def body(
    tok_hbm, wg_hbm, wu_hbm, wd_hbm, out_hbm,
    gin_hbm, dg_hbm, du_hbm, dd_hbm,
    tg, w, px, rxt, rxf, rz, pz, rzz, rzt, rzf, az, ax, acc, stage, trans,
    go, gs, gc, ys, yt, yf, zs, zr, gout,
    send, recv, local,
):
    row, col = lax.axis_index("row"), lax.axis_index("col")
    y, zh, core = row // 8, (row // 2) % 4, row % 2
    zl, x = col // 4, col % 4

    def at_row(y_, zh_, core_):
        return {"row": (y_ * 4 + zh_) * 2 + core_, "col": col}

    def at_col(zl_, x_):
        return {"row": row, "col": zl_ * 4 + x_}

    y_up, y_dn = at_row((y + 1) % 4, zh, core), at_row((y + 3) % 4, zh, core)
    zh_at = [None] + [at_row(y, (zh + d) % 4, core) for d in (1, 2, 3)]
    twin = at_row(y, zh, 1 - core)
    x_up, x_dn = at_col(zl, (x + 1) % 4), at_col(zl, (x + 3) % 4)
    z_pair = at_col(1 - zl, x)
    partners = [y_up, y_dn, zh_at[1], zh_at[2], zh_at[3], twin, x_up, x_dn, z_pair]

    counts = {"remote": 0, "local": 0}
    remote = {}

    def push(key, src, dst, device):
        n = counts["remote"]
        counts["remote"] = n + 1
        copy = pltpu.make_async_remote_copy(
            src_ref=src, dst_ref=dst, send_sem=send.at[n], recv_sem=recv.at[n],
            device_id=device, device_id_type=pl.DeviceIdType.MESH,
        )
        copy.start()
        assert key not in remote
        remote[key] = copy

    def arrive(*keys):
        for key in keys:
            remote[key].wait_recv()

    def move(src, dst):
        n = counts["local"]
        counts["local"] = n + 1
        copy = pltpu.make_async_copy(src, dst, local.at[n])
        copy.start()
        return copy

    d_model = w.shape[-1]
    ffb = w.shape[-2]
    cut = -(-ffb // 32) * 16
    chunk = px.shape[-1]
    halves = (pl.ds(0, cut), pl.ds(cut, ffb - cut))
    n_tile = min(256, d_model)

    def hbm_rows(j, h):
        first = ((x + j) % 4) * (2 * ffb) + (zl if h == 0 else 1 - zl) * ffb
        return pl.ds(pl.multiple_of(first, 16), ffb)

    tok_in = [move(tok_hbm, tg.at[0, 0, 0, 0]), move(out_hbm, tg.at[1, 0, 0, 0])]
    w_in = [
        [move(src.at[hbm_rows(j, h)], w.at[k, j, h]) for j in range(4) for h in range(2)]
        for k, src in enumerate((wg_hbm, wu_hbm, wd_hbm))
    ]

    barrier = pltpu.get_barrier_semaphore()
    for partner in partners:
        pl.semaphore_signal(barrier, inc=1, device_id=partner, device_id_type=pl.DeviceIdType.MESH)
    for copy in tok_in:
        copy.wait()
    pl.semaphore_wait(barrier, len(partners))

    def gather_start(s):
        own = tg.at[s, 0, 0, 0]
        for d in (2, 1, 3):
            push(("az", s, d), own, tg.at[s, 0, 0, 4 - d], zh_at[d])
        push(("ac", s, 0), own, tg.at[s, 0, 1, 0], twin)

    def gather_z(s):
        arrive(("az", s, 1), ("az", s, 2), ("az", s, 3))
        push(("ay", s, 1), tg.at[s, 0, 0], tg.at[s, 3, 0], y_up)
        push(("ay", s, 3), tg.at[s, 0, 0], tg.at[s, 1, 0], y_dn)
        push(("ac", s, 1), tg.at[s, 0, 0, pl.ds(1, 3)], tg.at[s, 0, 1, pl.ds(1, 3)], twin)

    def gather_y(s):
        arrive(("ay", s, 1), ("ay", s, 3))
        push(("at", s, 1), tg.at[s, 3, 0, pl.ds(0, 2)], tg.at[s, 2, 0, pl.ds(0, 2)], y_up)
        push(("at", s, 3), tg.at[s, 1, 0, pl.ds(2, 2)], tg.at[s, 2, 0, pl.ds(2, 2)], y_dn)
        push(("af", s, 1), tg.at[s, 1, 0], tg.at[s, 1, 1], twin)
        push(("af", s, 3), tg.at[s, 3, 0], tg.at[s, 3, 1], twin)

    def gather_t(s):
        arrive(("at", s, 1), ("at", s, 3))
        push(("af", s, 2), tg.at[s, 2, 0], tg.at[s, 2, 1], twin)

    def gathered(s, i):
        if i == 0:
            arrive(("ac", s, 0), ("ac", s, 1))
        else:
            arrive(("af", s, i))

    def rows_of(s, i):
        return tg[s, i].reshape(chunk, d_model)

    def product(k, s, i, pair):
        part = w[k, 2 * pair:2 * pair + 2].reshape(4 * ffb, d_model)
        out = mm(part, rows_of(s, i), ((1,), (1,)))
        return out.astype(BF16).reshape(2, 2, ffb, chunk)

    def gate_up_start(i):
        if i == 0:
            for copy in w_in[0] + w_in[1]:
                copy.wait()
        gathered(0, i)
        for pair in (1, 0):
            for k in (0, 1):
                px[i, 2 * pair:2 * pair + 2, :, k] = product(k, 0, i, pair)
            if pair == 1:
                push(("xt", i, 0), px.at[i, 2, 0], rxt.at[i, 0], x_up)
                push(("xt", i, 1), px.at[i, 2, 1], rxt.at[i, 1], x_dn)
                push(("xf", i, 1, 0), px.at[i, 3, 0], rxf.at[i, 1, 0], x_dn)
            else:
                push(("xf", i, 0, 1), px.at[i, 1, 1], rxf.at[i, 0, 1], x_up)

    def gate_up_pass(i):
        arrive(("xt", i, 0))
        px[i, 1, 0] = (px[i, 1, 0].astype(F32) + rxt[i, 0].astype(F32)).astype(BF16)
        push(("xf", i, 0, 0), px.at[i, 1, 0], rxf.at[i, 0, 0], x_up)
        arrive(("xt", i, 1))
        px[i, 3, 1] = (px[i, 3, 1].astype(F32) + rxt[i, 1].astype(F32)).astype(BF16)
        push(("xf", i, 1, 1), px.at[i, 3, 1], rxf.at[i, 1, 1], x_dn)

    def gate_up_sum(i, h):
        return px[i, 0, h].astype(F32) + rxf[i, 0, h].astype(F32) + rxf[i, 1, h].astype(F32)

    def gate_up_cross(i):
        arrive(("xf", i, 0, 0), ("xf", i, 0, 1), ("xf", i, 1, 0), ("xf", i, 1, 1))
        px[i, 0, 1] = gate_up_sum(i, 1).astype(BF16)
        push(("xz", i), px.at[i, 0, 1], rz.at[i], z_pair)

    def hid_start(i):
        if i == 0:
            for copy in w_in[2]:
                copy.wait()
        gathered(1, i)
        for pair in (1, 0):
            out = product(2, 1, i, pair)
            for j in range(2):
                for h in range(2):
                    pz[i, h, 2 * pair + j] = out[j, h]
        push(("zz", i), pz.at[i, 1], rzz.at[i], z_pair)

    def hid_cross(i):
        arrive(("zz", i))
        pz[i, 0] = (pz[i, 0].astype(F32) + rzz[i].astype(F32)).astype(BF16)
        for ab, (to, back, far, near) in enumerate(((x_up, x_dn, 0, 3), (x_dn, x_up, 1, 1))):
            push(("zt", i, ab), pz.at[i, 0, 2, halves[ab]], rzt.at[i, halves[ab]], to)
        push(("zf", i, 1, 0), pz.at[i, 0, 3, halves[0]], rzf.at[i, 1, halves[0]], x_dn)
        push(("zf", i, 0, 1), pz.at[i, 0, 1, halves[1]], rzf.at[i, 0, halves[1]], x_up)

    def hid_pass(i):
        for ab, (j, to) in enumerate(((1, x_up), (3, x_dn))):
            arrive(("zt", i, ab))
            part = pz[i, 0, j, halves[ab]].astype(F32) + rzt[i, halves[ab]].astype(F32)
            pz[i, 0, j, halves[ab]] = part.astype(BF16)
            push(("zf", i, ab, ab), pz.at[i, 0, j, halves[ab]], rzf.at[i, ab, halves[ab]], to)

    def pointwise(i):
        arrive(("xz", i))
        pre = gate_up_sum(i, 0) + rz[i].astype(F32)
        gate_pre, up_pre = pre[0], pre[1]
        arrive(("zf", i, 0, 0), ("zf", i, 0, 1), ("zf", i, 1, 0), ("zf", i, 1, 1))
        hid_grad = pz[i, 0, 0].astype(F32) + rzf[i, 0].astype(F32) + rzf[i, 1].astype(F32)
        logistic = 1.0 / (1.0 + jnp.exp(-gate_pre))
        activated = gate_pre * logistic
        az[i, 0, 0, 0] = (hid_grad * up_pre * logistic * (1.0 + gate_pre * (1.0 - logistic))).astype(BF16)
        az[i, 0, 0, 1] = (hid_grad * activated).astype(BF16)
        push(("gz", i), az.at[i, 0, 0], az.at[i, 0, 1], z_pair)
        push(("gx", i, 0, 0), az.at[i, 0, 0], az.at[i, 3, 0], x_up)
        push(("gx", i, 1, 0), az.at[i, 0, 0], az.at[i, 1, 0], x_dn)
        ax[i, 0, 0] = (activated * up_pre).astype(BF16)
        push(("hx", i, 0), ax.at[i, 0, 0], ax.at[i, 0, 3], x_up)
        push(("hx", i, 1), ax.at[i, 0, 0], ax.at[i, 0, 1], x_dn)
        push(("hz", i, 0), ax.at[i, 0, 0], ax.at[i, 1, 0], z_pair)

    def spread_pair(i):
        arrive(("gz", i))
        push(("gx", i, 0, 1), az.at[i, 0, 1], az.at[i, 3, 1], x_up)
        push(("gx", i, 1, 1), az.at[i, 0, 1], az.at[i, 1, 1], x_dn)

    def spread_far(i):
        arrive(("hx", i, 0), ("hx", i, 1))
        push(("ht", i, 0), ax.at[i, 0, 3, halves[0]], ax.at[i, 0, 2, halves[0]], x_up)
        push(("ht", i, 1), ax.at[i, 0, 1, halves[1]], ax.at[i, 0, 2, halves[1]], x_dn)
        arrive(("gx", i, 0, 0))
        push(("gt", i, 0), az.at[i, 3, 0], az.at[i, 2, 0], x_up)
        push(("hz", i, 1), ax.at[i, 0, 1], ax.at[i, 1, 1], z_pair)
        push(("hz", i, 3), ax.at[i, 0, 3], ax.at[i, 1, 3], z_pair)
        arrive(("gx", i, 1, 1))
        push(("gt", i, 1), az.at[i, 1, 1], az.at[i, 2, 1], x_dn)

    def spread_last(i):
        arrive(("ht", i, 0), ("ht", i, 1))
        push(("hz", i, 2), ax.at[i, 0, 2], ax.at[i, 1, 2], z_pair)

    def input_rows(i):
        arrive(("gx", i, 1, 0), ("gx", i, 0, 1), ("gt", i, 0), ("gt", i, 1))
        for k in (0, 1):
            trans[k] = az[i, :, :, k].reshape(8 * ffb, chunk).T
        for n in range(d_model // n_tile):
            cols = pl.ds(n * n_tile, n_tile)
            out = sum(
                mm(trans[k], w[k, :, :, :, cols].reshape(8 * ffb, n_tile), ((1,), (0,)))
                for k in (0, 1)
            )
            go[i, :, cols] = out[:chunk // 2]
            gs[i, :, cols] = out[chunk // 2:].astype(BF16)
        push(("cc", i), gs.at[i], gc.at[i], twin)

    n_half = chunk // 4
    top, low = pl.ds(0, n_half), pl.ds(n_half, n_half)

    def input_fold(i):
        arrive(("cc", i))
        if i == 0:
            go[0] = go[0] + gc[0].astype(F32)
        elif i == 1:
            ys[1] = (go[1] + gc[1].astype(F32)).astype(BF16)
            push(("yf", 0, 1), ys.at[1, low], yf.at[0, low], y_up)
        elif i == 2:
            ys[2] = (go[2] + gc[2].astype(F32)).astype(BF16)
            push(("yt", 0), ys.at[2, top], yt.at[0], y_up)
            push(("yt", 1), ys.at[2, low], yt.at[1], y_dn)
        else:
            ys[3, top] = (go[3, top] + gc[3, top].astype(F32)).astype(BF16)
            push(("yf", 1, 0), ys.at[3, top], yf.at[1, top], y_dn)
            arrive(("yt", 1))
            ys[3, low] = (go[3, low] + gc[3, low].astype(F32) + yt[1].astype(F32)).astype(BF16)
            push(("yf", 1, 1), ys.at[3, low], yf.at[1, low], y_dn)
            arrive(("yt", 0))
            ys[1, top] = (ys[1, top].astype(F32) + yt[0].astype(F32)).astype(BF16)
            push(("yf", 0, 0), ys.at[1, top], yf.at[0, top], y_up)

    def input_own():
        arrive(("yf", 0, 0), ("yf", 0, 1), ("yf", 1, 0), ("yf", 1, 1))
        go[0] = go[0] + yf[0].astype(F32) + yf[1].astype(F32)
        piece = chunk // 8
        for d in (2, 1, 3):
            zs[d] = go[0, d * piece:(d + 1) * piece].astype(BF16)
            push(("zr", d), zs.at[d], zr.at[d], zh_at[d])

    def input_out():
        piece = chunk // 8
        arrive(("zr", 1), ("zr", 2), ("zr", 3))
        gout[...] = (
            go[0, :piece] + zr[1].astype(F32) + zr[2].astype(F32) + zr[3].astype(F32)
        ).astype(BF16)
        return move(gout, gin_hbm)

    scale = float(NY * chunk) ** -0.5
    writes = []

    def weight_rows(k, i):
        left = az[i, :, :, k] if k < 2 else None
        s = 0 if k < 2 else 1
        for pair in (0, 1):
            js = slice(2 * pair, 2 * pair + 2)
            if k < 2:
                left = az[i, js, :, k].reshape(4 * ffb, chunk)
            else:
                left = jnp.concatenate(
                    [ax[i, h, j] for j in (2 * pair, 2 * pair + 1) for h in (0, 1)], axis=0
                )
            for n in range(d_model // n_tile):
                cols = pl.ds(n * n_tile, n_tile)
                right = tg[s, i, :, :, :, cols].reshape(chunk, n_tile)
                out = mm(left, right, ((1,), (0,))).reshape(2, 2, ffb, n_tile)
                if i > 0:
                    out = out + acc[k, js, :, :, cols]
                if i < NY - 1:
                    acc[k, js, :, :, cols] = out
                else:
                    stage[k, js, :, :, cols] = (out * scale).astype(BF16)
            if i == NY - 1:
                out_hbm_k = (dg_hbm, du_hbm, dd_hbm)[k]
                for j in (2 * pair, 2 * pair + 1):
                    for h in range(2):
                        writes.append(move(stage.at[k, j, h], out_hbm_k.at[hbm_rows(j, h)]))

    def weight_gate_up(i):
        weight_rows(0, i)
        weight_rows(1, i)

    def weight_down(i):
        arrive(("hz", i, 0), ("hz", i, 1), ("hz", i, 2), ("hz", i, 3))
        weight_rows(2, i)

    gather_start(0)
    gather_start(1)
    gather_z(0)
    gate_up_start(0)
    gather_z(1)
    hid_start(0)
    gather_y(0)
    gate_up_pass(0)
    hid_cross(0)
    gather_y(1)
    gate_up_start(1)
    gate_up_cross(0)
    hid_start(1)
    hid_pass(0)
    gather_t(0)
    gather_t(1)
    gate_up_pass(1)
    hid_cross(1)
    pointwise(0)
    gate_up_start(2)
    gate_up_cross(1)
    spread_pair(0)
    hid_start(2)
    hid_pass(1)
    spread_far(0)
    gate_up_pass(2)
    hid_cross(2)
    pointwise(1)
    spread_last(0)
    gate_up_start(3)
    gate_up_cross(2)
    spread_pair(1)
    hid_start(3)
    hid_pass(2)
    input_rows(0)
    spread_far(1)
    gate_up_pass(3)
    hid_cross(3)
    pointwise(2)
    spread_last(1)
    input_fold(0)
    weight_gate_up(0)
    gate_up_cross(3)
    spread_pair(2)
    hid_pass(3)
    input_rows(1)
    spread_far(2)
    pointwise(3)
    spread_last(2)
    input_fold(1)
    weight_down(0)
    spread_pair(3)
    weight_gate_up(1)
    input_rows(2)
    spread_far(3)
    input_fold(2)
    weight_down(1)
    spread_last(3)
    weight_gate_up(2)
    input_rows(3)
    weight_down(2)
    input_fold(3)
    weight_gate_up(3)
    input_own()
    weight_down(3)
    writes.append(input_out())
    for copy in remote.values():
        copy.wait_send()
    for copy in writes:
        copy.wait()


def local(tokens, w_gate, w_up, w_down, grad_out):
    piece, d = tokens.shape
    ff = w_gate.shape[0]
    ffb, chunk = ff // 8, 8 * piece
    hbm = pl.BlockSpec(memory_space=pl.ANY)

    def vmem(*shape, dtype=BF16):
        return pltpu.VMEM(shape, dtype)

    scratch = [
        vmem(2, 4, 2, 4, piece, d),
        vmem(3, 4, 2, ffb, d),
        vmem(4, 4, 2, 2, ffb, chunk),
        vmem(4, 2, 2, ffb, chunk),
        vmem(4, 2, 2, 2, ffb, chunk),
        vmem(4, 2, ffb, chunk),
        vmem(4, 2, 4, ffb, chunk),
        vmem(4, 4, ffb, chunk),
        vmem(4, ffb, chunk),
        vmem(4, 2, ffb, chunk),
        vmem(4, 4, 2, 2, ffb, chunk),
        vmem(4, 2, 4, ffb, chunk),
        vmem(3, 4, 2, ffb, d, dtype=F32),
        vmem(3, 4, 2, ffb, d),
        vmem(2, chunk, 8 * ffb),
        vmem(4, chunk // 2, d, dtype=F32),
        vmem(4, chunk // 2, d),
        vmem(4, chunk // 2, d),
        vmem(4, chunk // 2, d),
        vmem(2, chunk // 4, d),
        vmem(2, chunk // 2, d),
        vmem(4, piece, d),
        vmem(4, piece, d),
        vmem(piece, d),
        pltpu.SemaphoreType.DMA((160,)),
        pltpu.SemaphoreType.DMA((160,)),
        pltpu.SemaphoreType.DMA((56,)),
    ]
    weight = jax.ShapeDtypeStruct((ff, d), BF16)
    return pl.pallas_call(
        body,
        out_shape=(jax.ShapeDtypeStruct((piece, d), BF16), weight, weight, weight),
        in_specs=[hbm] * 5,
        out_specs=(hbm,) * 4,
        scratch_shapes=scratch,
        compiler_params=pltpu.CompilerParams(
            collective_id=0, has_side_effects=True, vmem_limit_bytes=60 * 2 ** 20
        ),
        cost_estimate=pl.CostEstimate(
            flops=16 * 4 * chunk * ff * d, bytes_accessed=12 * ff * d, transcendentals=4 * chunk * ffb
        ),
    )(tokens, w_gate, w_up, w_down, grad_out)


def solution(mesh):
    spec = P("row", "col")
    return jax.shard_map(
        local, mesh=mesh, in_specs=(spec,) * 5, out_specs=(spec,) * 4, check_vma=False
    )
```

time: 496 us -> 135 us (0.27)
  waiting for transfers between devices: 434 us -> 0 us
  Pallas kernels: 0 us -> 126 us
  matrix products: 43.9 us -> 0 us
  between operations: 13.9 us -> 0.64 us
  local copies, waits for them, and re-layouts: 0.02 us -> 7.87 us
    all_gather x5 -> x0, waiting for transfers between devices: 218 us -> none  [the longest x1 60.9 us: local(): lax.all_gather(grad_out, 'row', axis=0, tiled=True)]
    reduce_scatter x4 -> x0, waiting for transfers between devices: 213 us -> none  [the longest x1 93.2 us: local(): lax.psum_scatter(input_rows.astype(jnp.bfloat16), 'row', scatter_dimensio...]
    pallas_call x0 -> x1, Pallas kernels: none -> 126 us  [local(): pl.pallas_call(body, out_shape=(jax.ShapeDtypeStruct((piece, d), BF16), w...]
    dot_general x8 -> x0, matrix products: 43.9 us -> none  [the longest x3 16.7 us: col_partial(): lax.dot_general(operand, weight, (((1,), (1,)), ((), ())), preferred_elem...]
    unnamed x6 -> x8, local copies, waits for them, and re-layouts: 0.02 us -> 7.87 us
  transfers between devices with their start and end apart: 9 -> 0, of which waited for: 9 -> 0; matrix products, arithmetic and copies ran while one was open for 9% -> 0% of each run, Pallas kernels for 0% -> 0%
where the time goes in v1:
time: 135 us; the launch traced here: 134 us
  Pallas kernels  126 us (93%)
  local copies, waits for them, and re-layouts  7.87 us (6%)
    pallas_call x1, Pallas kernels, local(): pl.pallas_call(body, out_shape=(jax.ShapeDtypeStruct((piece, d), BF16), w...  126 us
    unnamed x8, local copies, waits for them, and re-layouts  7.87 us

profile of v1, /device:TPU:1, one launch (start us, length us, event | category | flops | bytes accessed | tf_op | source)
XLA Modules:
  0.0 134.1 jit_solution(13769470165721633072)
XLA Ops:
  0.6 125.6 %shard_map.84 = (bf16[32,1024]{1,0:T(8,128)(2,1)}, bf16[896,1024]{1,0:T(8,128)(2,1)}, bf16[896,1024]{1,0:T(8,128)(2,1)}, bf16[896,1024]{1,0:T(8,128)(2,1)}) custom-call(bf16[32,1024]{1,0:T(8,128)(2,1)} %tok_hbm.1, bf16[896,1024]{1,0:T(8,128)(2,1)} %wg_hbm.1, bf16[896,1024]{1,0:T(8,128)(2,1)} %wu_hbm.1, bf16[896,1024]{1,0:T(8,128)(2,1)} %wd_hbm.1, ...), custom_call_target="tpu_custom_call" | custom-call | flops 15032385536 | bytes 11010048 | tf_op jit(solution)/shard_map/pallas_call | solution.py:425
  126.2 1.5 %copy.13 = bf16[32,1024]{1,0:T(8,128)(2,1)} copy(bf16[32,1024]{1,0:T(8,128)(2,1)} %get-tuple-element.8) | data formatting | bytes 131072
  127.7 0.0 copy-start.1
  127.7 3.0 %copy.14 = bf16[896,1024]{1,0:T(8,128)(2,1)} copy(bf16[896,1024]{1,0:T(8,128)(2,1)} %get-tuple-element.9) | data formatting | bytes 3670016
  130.7 0.0 copy-done.1
  130.7 0.0 copy-start
  130.7 1.2 copy.15
  131.9 0.9 copy-done
  132.9 1.2 copy.16
Async XLA Ops:
  127.7 3.0 %copy-start.1 = (bf16[896,1024]{1,0:T(8,128)(2,1)S(1)}, bf16[896,1024]{1,0:T(8,128)(2,1)}, u32[]{:S(2)}) copy-start(bf16[896,1024]{1,0:T(8,128)(2,1)} %get-tuple-element.10) | copy-start | bytes 5505028
  130.7 2.2 %copy-start = (bf16[896,1024]{1,0:T(8,128)(2,1)S(1)}, bf16[896,1024]{1,0:T(8,128)(2,1)}, u32[]{:S(2)}) copy-start(bf16[896,1024]{1,0:T(8,128)(2,1)} %get-tuple-element.11) | copy-start | bytes 5505028

commit v2 on v1

v2 whole, which is shorter than its diff:
```python
import jax
import jax.numpy as jnp
from jax import lax
from jax.experimental import pallas as pl
from jax.experimental.pallas import tpu as pltpu
from jax.sharding import PartitionSpec as P

NY, NZ, NX = 4, 4, 4
F32, BF16 = jnp.float32, jnp.bfloat16
HAND_PARTS = 4


def mm(a, b, dims):
    return lax.dot_general(a, b, (dims, ((), ())), preferred_element_type=F32)


def body(
    tok_hbm, wg_hbm, wu_hbm, wd_hbm, out_hbm,
    gin_hbm, dg_hbm, du_hbm, dd_hbm,
    tg, w, px, rxt, rxf, rz, pz, rzz, rzt, rzf, az, ax, acc, stage, trans,
    part, gs, gc, ys, yt, yf, zs, zq, zr, gout,
    send, recv, local,
):
    row, col = lax.axis_index("row"), lax.axis_index("col")
    y, zh, core = row // 8, (row // 2) % 4, row % 2
    zl, x = col // 4, col % 4

    def at_row(y_, zh_, core_):
        return {"row": (y_ * 4 + zh_) * 2 + core_, "col": col}

    def at_col(zl_, x_):
        return {"row": row, "col": zl_ * 4 + x_}

    y_up, y_dn = at_row((y + 1) % 4, zh, core), at_row((y + 3) % 4, zh, core)
    zh_up, zh_dn = at_row(y, (zh + 1) % 4, core), at_row(y, (zh + 3) % 4, core)
    twin = at_row(y, zh, 1 - core)
    x_up, x_dn = at_col(zl, (x + 1) % 4), at_col(zl, (x + 3) % 4)
    z_pair = at_col(1 - zl, x)
    partners = [y_up, y_dn, zh_up, zh_dn, twin, x_up, x_dn, z_pair]

    sends, groups, arrived = {}, {}, set()
    sent_refs = {
        "xt": rxt, "xf": rxf, "xz": rz, "zz": rzz, "zt": rzt, "zf": rzf,
        "gz": az.at[:, 0, 1], "gx0": az.at[:, 3], "gx1": az.at[:, 1], "gt": az.at[:, 2],
        "hx0": ax.at[:, 0, 3], "hx1": ax.at[:, 0, 1], "ht": ax.at[:, 0, 2], "hz": ax.at[:, 1],
        "cc": gc, "yt": yt, "yf": yf, "zq": zq, "zr": zr,
        "az1": tg.at[3, 0, 0], "az3": tg.at[1, 0, 0], "at": tg.at[2, 0, 0],
        "ay1": tg.at[:, 0, 3], "ay3": tg.at[:, 0, 1], "ax": tg.at[:, 0, 2], "ac": tg.at[:, 1],
    }

    def copy_of(src, dst, send_at, recv_at, device):
        return pltpu.make_async_remote_copy(
            src_ref=src, dst_ref=dst, send_sem=send.at[send_at], recv_sem=recv.at[recv_at],
            device_id=device, device_id_type=pl.DeviceIdType.MESH,
        )

    def push(key, src, dst, device, whole=None):
        send_at = sends.setdefault(key[0], len(sends))
        recv_at, _ = groups.setdefault(key, (len(groups), dst if whole is None else whole))
        copy_of(src, dst, send_at, recv_at, device).start()

    def arrive(*keys):
        for key in keys:
            if key not in arrived:
                arrived.add(key)
                recv_at, whole = groups[key]
                copy_of(whole, whole, 0, recv_at, twin).wait_recv()

    def all_sent():
        for kind, send_at in sends.items():
            copy_of(sent_refs[kind], sent_refs[kind], send_at, 0, twin).wait_send()

    def move(n, src, dst):
        copy = pltpu.make_async_copy(src, dst, local.at[n])
        copy.start()
        return copy

    def moved(n, whole):
        pltpu.make_async_copy(whole, whole, local.at[n]).wait()

    d_model = w.shape[-1]
    ffb = w.shape[-2]
    cut = -(-ffb // 32) * 16
    chunk = px.shape[-1]
    halves = (pl.ds(0, cut), pl.ds(cut, ffb - cut))
    n_tile = min(256, d_model)

    def hbm_rows(j, h):
        first = ((x + j) % 4) * (2 * ffb) + (zl if h == 0 else 1 - zl) * ffb
        return pl.ds(pl.multiple_of(first, 16), ffb)

    tok_in = [move(6, tok_hbm, tg.at[0, 0, 0, 0]), move(7, out_hbm, tg.at[0, 0, 0, 1])]
    for k, src in enumerate((wg_hbm, wu_hbm, wd_hbm)):
        for j in range(4):
            for h in range(2):
                move(k, src.at[hbm_rows(j, h)], w.at[k, j, h])

    barrier = pltpu.get_barrier_semaphore()
    for partner in partners:
        pl.semaphore_signal(barrier, inc=1, device_id=partner, device_id_type=pl.DeviceIdType.MESH)
    for copy in tok_in:
        copy.wait()
    pl.semaphore_wait(barrier, len(partners))

    half = chunk // 16
    first, second = pl.ds(0, half), pl.ds(half, half)
    both = pl.ds(0, 2)

    def gather_start():
        for s in (0, 1):
            own = tg.at[0, 0, 0, s]
            push(("ay1", 0, s), own, tg.at[0, 0, 3, s], y_up)
            push(("ay3", 0, s), own, tg.at[0, 0, 1, s], y_dn)
            push(("ac", 0, s), own, tg.at[0, 1, 0, s], twin, tg.at[0, 1, :, s])
            push(("az1", s), own, tg.at[3, 0, 0, s], zh_up)
            push(("az3", s), own, tg.at[1, 0, 0, s], zh_dn)

    def gather_z():
        arrive(("az1", 0), ("az1", 1))
        push(("at",), tg.at[3, 0, 0, :, first], tg.at[2, 0, 0, :, first], zh_up, tg.at[2, 0, 0])
        arrive(("az3", 0), ("az3", 1))
        push(("at",), tg.at[1, 0, 0, :, second], tg.at[2, 0, 0, :, second], zh_dn, tg.at[2, 0, 0])

    def kind(c, s):
        return s if c < 2 else both

    def gather_y(c, s):
        if c == 1:
            arrive(("az3", s))
        elif c == 3:
            arrive(("az1", 0), ("az1", 1))
        else:
            arrive(("at",))
        own = tg.at[c, 0, 0, kind(c, s)]
        push(("ay1", c, s), own, tg.at[c, 0, 3, kind(c, s)], y_up)
        push(("ay3", c, s), own, tg.at[c, 0, 1, kind(c, s)], y_dn)

    def gather_far(c, s):
        far = tg.at[c, 0, 2, kind(c, s)]
        arrive(("ay1", c, s))
        push(("ax", c, s), tg.at[c, 0, 3, kind(c, s), first], tg.at[c, 0, 2, kind(c, s), first], y_up, far)
        arrive(("ay3", c, s))
        push(("ax", c, s), tg.at[c, 0, 1, kind(c, s), second], tg.at[c, 0, 2, kind(c, s), second], y_dn, far)
        if c == 0:
            for yr in (1, 3):
                push(("ac", c, s), tg.at[c, 0, yr, s], tg.at[c, 1, yr, s], twin, tg.at[0, 1, :, s])

    def gather_twin(c, s):
        arrive(("ax", c, s))
        if c == 0:
            push(("ac", c, s), tg.at[c, 0, 2, s], tg.at[c, 1, 2, s], twin, tg.at[0, 1, :, s])
        else:
            push(("ac", c, s), tg.at[c, 0, :, kind(c, s)], tg.at[c, 1, :, kind(c, s)], twin)

    def gathered(s, c):
        arrive(("ac", c, s if c < 2 else 0))

    def rows_of(s, c):
        return tg[c, :, :, s].reshape(chunk, d_model)

    def product(k, s, i, pair):
        part = w[k, 2 * pair:2 * pair + 2].reshape(4 * ffb, d_model)
        out = mm(part, rows_of(s, i), ((1,), (1,)))
        return out.astype(BF16).reshape(2, 2, ffb, chunk)

    def gate_up_start(i):
        if i == 0:
            moved(0, w.at[0])
            moved(1, w.at[1])
        gathered(0, i)
        for pair in (1, 0):
            for k in (0, 1):
                px[i, 2 * pair:2 * pair + 2, :, k] = product(k, 0, i, pair)
            if pair == 1:
                push(("xt", i), px.at[i, 2, 0], rxt.at[i, 0], x_up, rxt.at[i])
                push(("xt", i), px.at[i, 2, 1], rxt.at[i, 1], x_dn, rxt.at[i])
                push(("xf", i), px.at[i, 3, 0], rxf.at[i, 1, 0], x_dn, rxf.at[i])
            else:
                push(("xf", i), px.at[i, 1, 1], rxf.at[i, 0, 1], x_up, rxf.at[i])

    def gate_up_pass(i):
        arrive(("xt", i))
        px[i, 1, 0] = (px[i, 1, 0].astype(F32) + rxt[i, 0].astype(F32)).astype(BF16)
        push(("xf", i), px.at[i, 1, 0], rxf.at[i, 0, 0], x_up, rxf.at[i])
        px[i, 3, 1] = (px[i, 3, 1].astype(F32) + rxt[i, 1].astype(F32)).astype(BF16)
        push(("xf", i), px.at[i, 3, 1], rxf.at[i, 1, 1], x_dn, rxf.at[i])

    def gate_up_sum(i, h):
        return px[i, 0, h].astype(F32) + rxf[i, 0, h].astype(F32) + rxf[i, 1, h].astype(F32)

    def gate_up_cross(i):
        arrive(("xf", i))
        px[i, 0, 1] = gate_up_sum(i, 1).astype(BF16)
        push(("xz", i), px.at[i, 0, 1], rz.at[i], z_pair)

    def hid_start(i):
        if i == 0:
            moved(2, w.at[2])
        gathered(1, i)
        for pair in (1, 0):
            out = product(2, 1, i, pair)
            for j in range(2):
                for h in range(2):
                    pz[i, h, 2 * pair + j] = out[j, h]
        push(("zz", i), pz.at[i, 1], rzz.at[i], z_pair)

    def hid_cross(i):
        arrive(("zz", i))
        pz[i, 0] = (pz[i, 0].astype(F32) + rzz[i].astype(F32)).astype(BF16)
        for ab, (to, back, far, near) in enumerate(((x_up, x_dn, 0, 3), (x_dn, x_up, 1, 1))):
            push(("zt", i), pz.at[i, 0, 2, halves[ab]], rzt.at[i, halves[ab]], to, rzt.at[i])
        push(("zf", i), pz.at[i, 0, 3, halves[0]], rzf.at[i, 1, halves[0]], x_dn, rzf.at[i])
        push(("zf", i), pz.at[i, 0, 1, halves[1]], rzf.at[i, 0, halves[1]], x_up, rzf.at[i])

    def hid_pass(i):
        arrive(("zt", i))
        for ab, (j, to) in enumerate(((1, x_up), (3, x_dn))):
            part = pz[i, 0, j, halves[ab]].astype(F32) + rzt[i, halves[ab]].astype(F32)
            pz[i, 0, j, halves[ab]] = part.astype(BF16)
            push(("zf", i), pz.at[i, 0, j, halves[ab]], rzf.at[i, ab, halves[ab]], to, rzf.at[i])

    def pointwise(i):
        arrive(("xz", i))
        pre = gate_up_sum(i, 0) + rz[i].astype(F32)
        gate_pre, up_pre = pre[0], pre[1]
        arrive(("zf", i))
        hid_grad = pz[i, 0, 0].astype(F32) + rzf[i, 0].astype(F32) + rzf[i, 1].astype(F32)
        logistic = 1.0 / (1.0 + jnp.exp(-gate_pre))
        activated = gate_pre * logistic
        az[i, 0, 0, 0] = (hid_grad * up_pre * logistic * (1.0 + gate_pre * (1.0 - logistic))).astype(BF16)
        az[i, 0, 0, 1] = (hid_grad * activated).astype(BF16)
        push(("gz", i), az.at[i, 0, 0], az.at[i, 0, 1], z_pair)
        push(("gx0", i, 0), az.at[i, 0, 0], az.at[i, 3, 0], x_up)
        push(("gx1", i, 0), az.at[i, 0, 0], az.at[i, 1, 0], x_dn)
        ax[i, 0, 0] = (activated * up_pre).astype(BF16)

    def spread_pair(i):
        arrive(("gz", i))
        push(("gx0", i, 1), az.at[i, 0, 1], az.at[i, 3, 1], x_up)
        push(("gx1", i, 1), az.at[i, 0, 1], az.at[i, 1, 1], x_dn)

    def spread_far(i):
        arrive(("gx0", i, 0))
        push(("gt", i), az.at[i, 3, 0], az.at[i, 2, 0], x_up, az.at[i, 2])
        arrive(("gx1", i, 1))
        push(("gt", i), az.at[i, 1, 1], az.at[i, 2, 1], x_dn, az.at[i, 2])

    def down_start(i):
        push(("hx0", i), ax.at[i, 0, 0], ax.at[i, 0, 3], x_up)
        push(("hx1", i), ax.at[i, 0, 0], ax.at[i, 0, 1], x_dn)
        push(("hz", i), ax.at[i, 0, 0], ax.at[i, 1, 0], z_pair, ax.at[i, 1])

    def down_far(i):
        arrive(("hx0", i))
        push(("ht", i), ax.at[i, 0, 3, halves[0]], ax.at[i, 0, 2, halves[0]], x_up, ax.at[i, 0, 2])
        push(("hz", i), ax.at[i, 0, 3], ax.at[i, 1, 3], z_pair, ax.at[i, 1])
        arrive(("hx1", i))
        push(("ht", i), ax.at[i, 0, 1, halves[1]], ax.at[i, 0, 2, halves[1]], x_dn, ax.at[i, 0, 2])
        push(("hz", i), ax.at[i, 0, 1], ax.at[i, 1, 1], z_pair, ax.at[i, 1])

    def down_last(i):
        arrive(("ht", i))
        push(("hz", i), ax.at[i, 0, 2], ax.at[i, 1, 2], z_pair, ax.at[i, 1])

    def input_near(i):
        arrive(("gz", i), ("gx0", i, 0), ("gx1", i, 1), ("gx1", i, 0), ("gx0", i, 1))
        for j in (0, 1, 3):
            for k in (0, 1):
                trans[k, j] = az[i, j, :, k].reshape(2 * ffb, chunk).T
        for n in range(d_model // n_tile):
            cols = pl.ds(n * n_tile, n_tile)
            part[i, :, cols] = sum(
                mm(trans[k, j], w[k, j, :, :, cols].reshape(2 * ffb, n_tile), ((1,), (0,)))
                for k in (0, 1) for j in (0, 1, 3)
            )

    def input_rows(i):
        arrive(("gt", i))
        for k in (0, 1):
            trans[k, 2] = az[i, 2, :, k].reshape(2 * ffb, chunk).T
        for n in range(d_model // n_tile):
            cols = pl.ds(n * n_tile, n_tile)
            out = part[i, :, cols] + sum(
                mm(trans[k, 2], w[k, 2, :, :, cols].reshape(2 * ffb, n_tile), ((1,), (0,)))
                for k in (0, 1)
            )
            part[i, :chunk // 2, cols] = out[:chunk // 2]
            gs[i, :, cols] = out[chunk // 2:].astype(BF16)
        push(("cc", i), gs.at[i], gc.at[i], twin)

    piece = chunk // 8

    def at_y(yr):
        return pl.ds(yr * piece, piece)

    def input_fold(i):
        arrive(("cc", i))
        part[i, at_y(0)] = part[i, at_y(0)] + gc[i, at_y(0)].astype(F32)
        for yr in (2, 1, 3):
            ys[i, yr] = (part[i, at_y(yr)] + gc[i, at_y(yr)].astype(F32)).astype(BF16)
            if yr == 2:
                push(("yt", i), ys.at[i, 2, first], yt.at[i, first], y_up, yt.at[i])
                push(("yt", i), ys.at[i, 2, second], yt.at[i, second], y_dn, yt.at[i])
            elif yr == 1:
                push(("yf", i), ys.at[i, 1, second], yf.at[i, 0, second], y_up, yf.at[i])
            else:
                push(("yf", i), ys.at[i, 3, first], yf.at[i, 1, first], y_dn, yf.at[i])

    def input_pass(i):
        arrive(("yt", i))
        for ab, (yr, rows, to) in enumerate(((1, first, y_up), (3, second, y_dn))):
            ys[i, yr, rows] = (ys[i, yr, rows].astype(F32) + yt[i, rows].astype(F32)).astype(BF16)
            push(("yf", i), ys.at[i, yr, rows], yf.at[i, ab, rows], to, yf.at[i])

    def input_own(i):
        arrive(("yf", i))
        part[i, at_y(0)] = part[i, at_y(0)] + yf[i, 0].astype(F32) + yf[i, 1].astype(F32)
        if i == 1:
            zs[1, second] = part[1, pl.ds(half, half)].astype(BF16)
            push(("zr",), zs.at[1, second], zr.at[0, second], zh_up, zr)
        elif i == 2:
            zs[2] = part[2, at_y(0)].astype(BF16)
            push(("zq",), zs.at[2, first], zq.at[first], zh_up, zq)
            push(("zq",), zs.at[2, second], zq.at[second], zh_dn, zq)
        elif i == 3:
            arrive(("zq",))
            zs[3, first] = part[3, pl.ds(0, half)].astype(BF16)
            zs[3, second] = (part[3, pl.ds(half, half)] + zq[second].astype(F32)).astype(BF16)
            push(("zr",), zs.at[3], zr.at[1], zh_dn, zr)

    def input_far():
        arrive(("zq",))
        zs[1, first] = (part[1, pl.ds(0, half)] + zq[first].astype(F32)).astype(BF16)
        push(("zr",), zs.at[1, first], zr.at[0, first], zh_up, zr)

    def input_out():
        arrive(("zr",))
        gout[...] = (
            part[0, at_y(0)] + zr[0].astype(F32) + zr[1].astype(F32)
        ).astype(BF16)
        move(6, gout, gin_hbm)

    scale = float(NY * chunk) ** -0.5

    def weight_rows(k, i):
        s = 0 if k < 2 else 1
        for pair in (0, 1):
            js = slice(2 * pair, 2 * pair + 2)
            if k < 2:
                left = az[i, js, :, k].reshape(4 * ffb, chunk)
            else:
                left = jnp.concatenate(
                    [ax[i, h, j] for j in (2 * pair, 2 * pair + 1) for h in (0, 1)], axis=0
                )
            for n in range(d_model // n_tile):
                cols = pl.ds(n * n_tile, n_tile)
                right = tg[i, :, :, s, :, cols].reshape(chunk, n_tile)
                out = mm(left, right, ((1,), (0,))).reshape(2, 2, ffb, n_tile)
                if i > 0:
                    out = out + acc[k, js, :, :, cols]
                if i < NY - 1:
                    acc[k, js, :, :, cols] = out
                else:
                    stage[k, js, :, :, cols] = (out * scale).astype(BF16)
            if i == NY - 1:
                out_hbm_k = (dg_hbm, du_hbm, dd_hbm)[k]
                for j in (2 * pair, 2 * pair + 1):
                    for h in range(2):
                        move(3 + k, stage.at[k, j, h], out_hbm_k.at[hbm_rows(j, h)])

    def weight_pair(i):
        weight_rows(0, i)
        weight_rows(1, i)

    def weight_down(i):
        arrive(("hz", i))
        weight_rows(2, i)

    gather_start()
    gather_far(0, 0)
    gather_far(0, 1)
    gather_twin(0, 0)
    gather_y(1, 0)
    gate_up_start(0)
    gather_z()
    gather_twin(0, 1)
    gather_far(1, 0)
    gather_y(1, 1)
    gather_y(3, 0)
    gather_twin(1, 0)
    gate_up_pass(0)
    gather_far(1, 1)
    hid_start(0)
    gate_up_start(1)
    gather_far(3, 0)
    gather_y(2, 0)
    gather_twin(1, 1)
    gate_up_pass(1)
    hid_start(1)
    gather_twin(3, 0)
    gather_far(2, 0)
    hid_cross(0)
    gate_up_start(3)
    gate_up_cross(1)
    gather_twin(2, 0)
    hid_cross(1)
    hid_start(3)
    gate_up_start(2)
    hid_pass(1)
    hid_start(2)
    gate_up_pass(2)
    gate_up_cross(0)
    gate_up_pass(3)
    pointwise(1)
    gate_up_cross(2)
    hid_pass(0)
    gate_up_cross(3)
    hid_cross(3)
    hid_cross(2)
    pointwise(0)
    hid_pass(2)
    hid_pass(3)
    spread_pair(1)
    pointwise(2)
    down_start(0)
    spread_pair(2)
    spread_far(1)
    input_near(1)
    down_start(1)
    spread_far(2)
    pointwise(3)
    input_near(2)
    spread_pair(3)
    down_far(0)
    input_rows(1)
    input_fold(1)
    down_start(3)
    input_rows(2)
    down_far(1)
    input_fold(2)
    input_pass(1)
    spread_far(3)
    down_last(0)
    input_pass(2)
    spread_pair(0)
    input_own(1)
    input_near(3)
    down_last(1)
    weight_down(0)
    input_own(2)
    input_rows(3)
    down_start(2)
    spread_far(0)
    down_far(3)
    input_fold(3)
    weight_down(1)
    down_far(2)
    input_near(0)
    input_far()
    input_pass(3)
    input_rows(0)
    weight_pair(0)
    input_own(3)
    down_last(2)
    input_fold(0)
    weight_pair(1)
    down_last(3)
    weight_pair(2)
    input_pass(0)
    weight_pair(3)
    weight_down(2)
    weight_down(3)
    input_own(0)
    input_out()
    assert arrived == set(groups)
    all_sent()
    for k in range(3):
        moved(3 + k, stage.at[k])
    moved(6, gout)


def hand_over(*refs):
    sems = refs[-1]
    inward, outward = [], []
    for n in (1, 2, 3, 0):
        src, dst, mid = refs[n], refs[4 + n], refs[8 + n]
        rows = src.shape[0]
        parts = HAND_PARTS if n else 1
        for p in range(parts):
            at = pl.ds(p * (rows // parts), rows // parts)
            inward.append(pltpu.make_async_copy(src.at[at], mid.at[at], sems.at[0, n, p]))
            outward.append(pltpu.make_async_copy(mid.at[at], dst.at[at], sems.at[1, n, p]))
    for copy in inward:
        copy.start()
    for arrived, copy in zip(inward, outward):
        arrived.wait()
        copy.start()
    for copy in outward:
        copy.wait()


def local(tokens, w_gate, w_up, w_down, grad_out):
    piece, d = tokens.shape
    ff = w_gate.shape[0]
    ffb, chunk = ff // 8, 8 * piece
    hbm = pl.BlockSpec(memory_space=pl.ANY)

    def vmem(*shape, dtype=BF16):
        return pltpu.VMEM(shape, dtype)

    scratch = [
        vmem(4, 2, 4, 2, piece, d),
        vmem(3, 4, 2, ffb, d),
        vmem(4, 4, 2, 2, ffb, chunk),
        vmem(4, 2, 2, ffb, chunk),
        vmem(4, 2, 2, 2, ffb, chunk),
        vmem(4, 2, ffb, chunk),
        vmem(4, 2, 4, ffb, chunk),
        vmem(4, 4, ffb, chunk),
        vmem(4, ffb, chunk),
        vmem(4, 2, ffb, chunk),
        vmem(4, 4, 2, 2, ffb, chunk),
        vmem(4, 2, 4, ffb, chunk),
        vmem(3, 4, 2, ffb, d, dtype=F32),
        vmem(3, 4, 2, ffb, d),
        vmem(2, 4, chunk, 2 * ffb),
        vmem(4, chunk, d, dtype=F32),
        vmem(4, chunk // 2, d),
        vmem(4, chunk // 2, d),
        vmem(4, 4, piece, d),
        vmem(4, piece, d),
        vmem(4, 2, piece, d),
        vmem(4, piece, d),
        vmem(piece, d),
        vmem(2, piece, d),
        vmem(piece, d),
        pltpu.SemaphoreType.DMA((26,)),
        pltpu.SemaphoreType.DMA((120,)),
        pltpu.SemaphoreType.DMA((8,)),
    ]
    weight = jax.ShapeDtypeStruct((ff, d), BF16)
    held = pl.pallas_call(
        body,
        out_shape=(jax.ShapeDtypeStruct((piece, d), BF16), weight, weight, weight),
        in_specs=[hbm] * 5,
        out_specs=(hbm,) * 4,
        scratch_shapes=scratch,
        compiler_params=pltpu.CompilerParams(
            collective_id=0, has_side_effects=True, vmem_limit_bytes=60 * 2 ** 20
        ),
        cost_estimate=pl.CostEstimate(
            flops=16 * 4 * chunk * ff * d, bytes_accessed=12 * ff * d, transcendentals=4 * chunk * ffb
        ),
    )(tokens, w_gate, w_up, w_down, grad_out)
    return pl.pallas_call(
        hand_over,
        out_shape=tuple(jax.ShapeDtypeStruct(one.shape, one.dtype) for one in held),
        in_specs=[hbm] * 4,
        out_specs=(hbm,) * 4,
        scratch_shapes=[vmem(*one.shape) for one in held] + [pltpu.SemaphoreType.DMA((2, 4, HAND_PARTS))],
        compiler_params=pltpu.CompilerParams(vmem_limit_bytes=60 * 2 ** 20),
        cost_estimate=pl.CostEstimate(flops=0, bytes_accessed=12 * ff * d, transcendentals=0),
    )(*held)


def solution(mesh):
    spec = P("row", "col")
    return jax.shard_map(
        local, mesh=mesh, in_specs=(spec,) * 5, out_specs=(spec,) * 4, check_vma=False
    )
```

time: 135 us -> 112 us (0.83)
  Pallas kernels: 126 us -> 111 us
  local copies, waits for them, and re-layouts: 7.87 us -> 0 us
    pallas_call x1, Pallas kernels: 126 us -> 106 us  [local(): pl.pallas_call(body, out_shape=(jax.ShapeDtypeStruct((piece, d), BF16), w...]
    unnamed x8 -> x0, local copies, waits for them, and re-layouts: 7.87 us -> none
    pallas_call x0 -> x1, Pallas kernels: none -> 5.1 us  [local(): pl.pallas_call(hand_over, out_shape=tuple((jax.ShapeDtypeStruct(one.shape...]
where the time goes in v2:
time: 112 us
  Pallas kernels  111 us (99%)
    pallas_call x1, Pallas kernels, local(): pl.pallas_call(body, out_shape=(jax.ShapeDtypeStruct((piece, d), BF16), w...  106 us
    pallas_call x1, Pallas kernels, local(): pl.pallas_call(hand_over, out_shape=tuple((jax.ShapeDtypeStruct(one.shape...  5.1 us

profile of v2, /device:TPU:1, one launch (start us, length us, event | category | flops | bytes accessed | tf_op | source)
XLA Modules:
  0.0 112.0 jit_solution(5910507226258506868)
XLA Ops:
  0.6 106.1 %shard_map.84 = (bf16[32,1024]{1,0:T(8,128)(2,1)}, bf16[896,1024]{1,0:T(8,128)(2,1)}, bf16[896,1024]{1,0:T(8,128)(2,1)}, bf16[896,1024]{1,0:T(8,128)(2,1)}) custom-call(bf16[32,1024]{1,0:T(8,128)(2,1)} %tok_hbm.1, bf16[896,1024]{1,0:T(8,128)(2,1)} %wg_hbm.1, bf16[896,1024]{1,0:T(8,128)(2,1)} %wu_hbm.1, bf16[896,1024]{1,0:T(8,128)(2,1)} %wd_hbm.1, ...), custom_call_target="tpu_custom_call" | custom-call | flops 15032385536 | bytes 11010048 | tf_op jit(solution)/shard_map/pallas_call | solution.py:542
  106.8 5.1 %shard_map.85 = (bf16[32,1024]{1,0:T(8,128)(2,1)}, bf16[896,1024]{1,0:T(8,128)(2,1)}, bf16[896,1024]{1,0:T(8,128)(2,1)}, bf16[896,1024]{1,0:T(8,128)(2,1)}) custom-call(bf16[32,1024]{1,0:T(8,128)(2,1)} %get-tuple-element.8.refs_0_, bf16[896,1024]{1,0:T(8,128)(2,1)} %get-tuple-element.9.refs_1_, bf16[896,1024]{1,0:T(8,128)(2,1)} %get-tuple-element.10.refs_2_, ...), custom_call_target="tpu_custom_call" | custom-call | bytes 11010048 | tf_op jit(solution)/shard_map/pallas_call | solution.py:555

commit v3 on v2

--- a/solution.py
+++ b/solution.py
@@ -7,7 +7,7 @@
 
 NY, NZ, NX = 4, 4, 4
 F32, BF16 = jnp.float32, jnp.bfloat16
-HAND_PARTS = 4
+HAND_PARTS = 1
 
 
 def mm(a, b, dims):
@@ -45,7 +45,7 @@
         "hx0": ax.at[:, 0, 3], "hx1": ax.at[:, 0, 1], "ht": ax.at[:, 0, 2], "hz": ax.at[:, 1],
         "cc": gc, "yt": yt, "yf": yf, "zq": zq, "zr": zr,
         "az1": tg.at[3, 0, 0], "az3": tg.at[1, 0, 0], "at": tg.at[2, 0, 0],
-        "ay1": tg.at[:, 0, 3], "ay3": tg.at[:, 0, 1], "ax": tg.at[:, 0, 2], "ac": tg.at[:, 1],
+        "ay1": tg.at[:, 3, 0], "ay3": tg.at[:, 1, 0], "ax": tg.at[:, 2, 0], "ac": tg.at[:, :, 1],
     }
 
     def copy_of(src, dst, send_at, recv_at, device):
@@ -109,9 +109,9 @@
     def gather_start():
         for s in (0, 1):
             own = tg.at[0, 0, 0, s]
-            push(("ay1", 0, s), own, tg.at[0, 0, 3, s], y_up)
-            push(("ay3", 0, s), own, tg.at[0, 0, 1, s], y_dn)
-            push(("ac", 0, s), own, tg.at[0, 1, 0, s], twin, tg.at[0, 1, :, s])
+            push(("ay1", 0, s), own, tg.at[0, 3, 0, s], y_up)
+            push(("ay3", 0, s), own, tg.at[0, 1, 0, s], y_dn)
+            push(("ac", 0, s, 0), own, tg.at[0, 0, 1, s], twin, tg.at[0, pl.ds(0, 2), 1, s])
             push(("az1", s), own, tg.at[3, 0, 0, s], zh_up)
             push(("az3", s), own, tg.at[1, 0, 0, s], zh_dn)
 
@@ -132,28 +132,37 @@
         else:
             arrive(("at",))
         own = tg.at[c, 0, 0, kind(c, s)]
-        push(("ay1", c, s), own, tg.at[c, 0, 3, kind(c, s)], y_up)
-        push(("ay3", c, s), own, tg.at[c, 0, 1, kind(c, s)], y_dn)
+        push(("ay1", c, s), own, tg.at[c, 3, 0, kind(c, s)], y_up)
+        push(("ay3", c, s), own, tg.at[c, 1, 0, kind(c, s)], y_dn)
+
+    def gather_near(c, s):
+        far = tg.at[c, 2, 0, kind(c, s)]
+        arrive(("ay3", c, s))
+        push(("ax", c, s), tg.at[c, 1, 0, kind(c, s), second], tg.at[c, 2, 0, kind(c, s), second], y_dn, far)
+        if c == 0:
+            push(("ac", 0, s, 0), tg.at[0, 1, 0, s], tg.at[0, 1, 1, s], twin, tg.at[0, pl.ds(0, 2), 1, s])
 
     def gather_far(c, s):
-        far = tg.at[c, 0, 2, kind(c, s)]
+        far = tg.at[c, 2, 0, kind(c, s)]
         arrive(("ay1", c, s))
-        push(("ax", c, s), tg.at[c, 0, 3, kind(c, s), first], tg.at[c, 0, 2, kind(c, s), first], y_up, far)
-        arrive(("ay3", c, s))
-        push(("ax", c, s), tg.at[c, 0, 1, kind(c, s), second], tg.at[c, 0, 2, kind(c, s), second], y_dn, far)
+        push(("ax", c, s), tg.at[c, 3, 0, kind(c, s), first], tg.at[c, 2, 0, kind(c, s), first], y_up, far)
         if c == 0:
-            for yr in (1, 3):
-                push(("ac", c, s), tg.at[c, 0, yr, s], tg.at[c, 1, yr, s], twin, tg.at[0, 1, :, s])
+            push(("ac", 0, s, 1), tg.at[0, 3, 0, s], tg.at[0, 3, 1, s], twin, tg.at[0, pl.ds(2, 2), 1, s])
+        else:
+            gather_near(c, s)
 
     def gather_twin(c, s):
         arrive(("ax", c, s))
         if c == 0:
-            push(("ac", c, s), tg.at[c, 0, 2, s], tg.at[c, 1, 2, s], twin, tg.at[0, 1, :, s])
+            push(("ac", 0, s, 1), tg.at[0, 2, 0, s], tg.at[0, 2, 1, s], twin, tg.at[0, pl.ds(2, 2), 1, s])
         else:
-            push(("ac", c, s), tg.at[c, 0, :, kind(c, s)], tg.at[c, 1, :, kind(c, s)], twin)
+            push(("ac", c, s), tg.at[c, :, 0, kind(c, s)], tg.at[c, :, 1, kind(c, s)], twin)
 
     def gathered(s, c):
-        arrive(("ac", c, s if c < 2 else 0))
+        if c == 0:
+            arrive(("ac", 0, s, 0), ("ac", 0, s, 1))
+        else:
+            arrive(("ac", c, s if c < 2 else 0))
 
     def rows_of(s, c):
         return tg[c, :, :, s].reshape(chunk, d_model)
@@ -163,10 +172,26 @@
         out = mm(part, rows_of(s, i), ((1,), (1,)))
         return out.astype(BF16).reshape(2, 2, ffb, chunk)
 
-    def gate_up_start(i):
-        if i == 0:
+    def gate_up_first(part_at):
+        if part_at == 0:
             moved(0, w.at[0])
             moved(1, w.at[1])
+        arrive(("ac", 0, 0, part_at))
+        lanes = pl.ds(part_at * (chunk // 2), chunk // 2)
+        rows = tg[0, 2 * part_at:2 * part_at + 2, :, 0].reshape(chunk // 2, d_model)
+        for pair in (1, 0):
+            for k in (0, 1):
+                weight = w[k, 2 * pair:2 * pair + 2].reshape(4 * ffb, d_model)
+                out = mm(weight, rows, ((1,), (1,))).astype(BF16)
+                px[0, 2 * pair:2 * pair + 2, :, k, :, lanes] = out.reshape(2, 2, ffb, chunk // 2)
+            if pair == 1:
+                push(("xt", 0), px.at[0, 2, 0, :, :, lanes], rxt.at[0, 0, :, :, lanes], x_up, rxt.at[0])
+                push(("xt", 0), px.at[0, 2, 1, :, :, lanes], rxt.at[0, 1, :, :, lanes], x_dn, rxt.at[0])
+                push(("xf", 0), px.at[0, 3, 0, :, :, lanes], rxf.at[0, 1, 0, :, :, lanes], x_dn, rxf.at[0])
+            else:
+                push(("xf", 0), px.at[0, 1, 1, :, :, lanes], rxf.at[0, 0, 1, :, :, lanes], x_up, rxf.at[0])
+
+    def gate_up_start(i):
         gathered(0, i)
         for pair in (1, 0):
             for k in (0, 1):
@@ -284,20 +309,24 @@
                 mm(trans[k, 2], w[k, 2, :, :, cols].reshape(2 * ffb, n_tile), ((1,), (0,)))
                 for k in (0, 1)
             )
-            part[i, :chunk // 2, cols] = out[:chunk // 2]
-            gs[i, :, cols] = out[chunk // 2:].astype(BF16)
+            part[i, :, cols] = out
+            other = out.reshape(4, 2, piece, n_tile)[:, 1].reshape(chunk // 2, n_tile)
+            gs[i, :, cols] = other.astype(BF16)
         push(("cc", i), gs.at[i], gc.at[i], twin)
 
     piece = chunk // 8
 
     def at_y(yr):
+        return pl.ds(yr * 2 * piece, piece)
+
+    def at_other(yr):
         return pl.ds(yr * piece, piece)
 
     def input_fold(i):
         arrive(("cc", i))
-        part[i, at_y(0)] = part[i, at_y(0)] + gc[i, at_y(0)].astype(F32)
+        part[i, at_y(0)] = part[i, at_y(0)] + gc[i, at_other(0)].astype(F32)
         for yr in (2, 1, 3):
-            ys[i, yr] = (part[i, at_y(yr)] + gc[i, at_y(yr)].astype(F32)).astype(BF16)
+            ys[i, yr] = (part[i, at_y(yr)] + gc[i, at_other(yr)].astype(F32)).astype(BF16)
             if yr == 2:
                 push(("yt", i), ys.at[i, 2, first], yt.at[i, first], y_up, yt.at[i])
                 push(("yt", i), ys.at[i, 2, second], yt.at[i, second], y_dn, yt.at[i])
@@ -342,7 +371,10 @@
 
     scale = float(NY * chunk) ** -0.5
 
+    added = [0, 0, 0]
+
     def weight_rows(k, i):
+        added[k] += 1
         s = 0 if k < 2 else 1
         for pair in (0, 1):
             js = slice(2 * pair, 2 * pair + 2)
@@ -356,13 +388,13 @@
                 cols = pl.ds(n * n_tile, n_tile)
                 right = tg[i, :, :, s, :, cols].reshape(chunk, n_tile)
                 out = mm(left, right, ((1,), (0,))).reshape(2, 2, ffb, n_tile)
-                if i > 0:
+                if added[k] > 1:
                     out = out + acc[k, js, :, :, cols]
-                if i < NY - 1:
+                if added[k] < NY:
                     acc[k, js, :, :, cols] = out
                 else:
                     stage[k, js, :, :, cols] = (out * scale).astype(BF16)
-            if i == NY - 1:
+            if added[k] == NY:
                 out_hbm_k = (dg_hbm, du_hbm, dd_hbm)[k]
                 for j in (2 * pair, 2 * pair + 1):
                     for h in range(2):
@@ -377,99 +409,102 @@
         weight_rows(2, i)
 
     gather_start()
+    gather_near(0, 0)
     gather_far(0, 0)
+    gate_up_first(0)
+    gather_y(1, 0)
+    gather_twin(0, 0)
     gather_far(0, 1)
-    gather_twin(0, 0)
-    gather_y(1, 0)
-    gate_up_start(0)
-    gather_z()
-    gather_twin(0, 1)
+    gather_near(0, 1)
+    gate_up_first(1)
     gather_far(1, 0)
     gather_y(1, 1)
+    gather_twin(0, 1)
+    gate_up_pass(0)
     gather_y(3, 0)
+    gather_z()
     gather_twin(1, 0)
-    gate_up_pass(0)
-    gather_far(1, 1)
     hid_start(0)
     gate_up_start(1)
+    gather_far(1, 1)
     gather_far(3, 0)
+    gather_twin(1, 1)
     gather_y(2, 0)
-    gather_twin(1, 1)
     gate_up_pass(1)
+    gather_twin(3, 0)
     hid_start(1)
-    gather_twin(3, 0)
-    gather_far(2, 0)
     hid_cross(0)
     gate_up_start(3)
+    gather_far(2, 0)
     gate_up_cross(1)
+    hid_start(3)
     gather_twin(2, 0)
+    gate_up_pass(3)
     hid_cross(1)
-    hid_start(3)
     gate_up_start(2)
     hid_pass(1)
     hid_start(2)
     gate_up_pass(2)
+    pointwise(1)
     gate_up_cross(0)
-    gate_up_pass(3)
-    pointwise(1)
+    hid_cross(2)
     gate_up_cross(2)
+    hid_cross(3)
+    gate_up_cross(3)
+    spread_pair(1)
+    hid_pass(3)
+    hid_pass(2)
+    down_start(1)
+    spread_far(1)
+    pointwise(2)
+    pointwise(3)
+    input_near(1)
+    spread_pair(2)
+    down_start(3)
+    down_far(1)
+    input_rows(1)
     hid_pass(0)
-    gate_up_cross(3)
-    hid_cross(3)
-    hid_cross(2)
+    input_fold(1)
+    spread_far(2)
+    spread_pair(3)
     pointwise(0)
-    hid_pass(2)
-    hid_pass(3)
-    spread_pair(1)
-    pointwise(2)
+    input_near(2)
+    input_rows(2)
+    input_pass(1)
+    down_far(3)
+    input_fold(2)
     down_start(0)
-    spread_pair(2)
-    spread_far(1)
-    input_near(1)
-    down_start(1)
-    spread_far(2)
-    pointwise(3)
-    input_near(2)
-    spread_pair(3)
+    spread_far(3)
+    spread_pair(0)
+    weight_pair(2)
+    input_own(1)
+    down_start(2)
+    down_last(1)
+    input_pass(2)
+    weight_pair(1)
+    input_near(3)
+    input_own(2)
+    down_last(3)
+    input_rows(3)
+    weight_pair(3)
+    spread_far(0)
     down_far(0)
-    input_rows(1)
-    input_fold(1)
-    down_start(3)
-    input_rows(2)
-    down_far(1)
-    input_fold(2)
-    input_pass(1)
-    spread_far(3)
-    down_last(0)
-    input_pass(2)
-    spread_pair(0)
-    input_own(1)
-    input_near(3)
-    down_last(1)
-    weight_down(0)
-    input_own(2)
-    input_rows(3)
-    down_start(2)
-    spread_far(0)
-    down_far(3)
     input_fold(3)
-    weight_down(1)
     down_far(2)
     input_near(0)
-    input_far()
     input_pass(3)
     input_rows(0)
+    down_last(0)
+    down_last(2)
+    input_own(3)
+    input_far()
+    input_fold(0)
     weight_pair(0)
-    input_own(3)
-    down_last(2)
-    input_fold(0)
-    weight_pair(1)
-    down_last(3)
-    weight_pair(2)
+    weight_down(3)
+    weight_down(1)
     input_pass(0)
-    weight_pair(3)
     weight_down(2)
-    weight_down(3)
+    weight_down(0)
     input_own(0)
     input_out()
     assert arrived == set(groups)
@@ -509,7 +544,7 @@
         return pltpu.VMEM(shape, dtype)
 
     scratch = [
-        vmem(4, 2, 4, 2, piece, d),
+        vmem(4, 4, 2, 2, piece, d),
         vmem(3, 4, 2, ffb, d),
         vmem(4, 4, 2, 2, ffb, chunk),
         vmem(4, 2, 2, ffb, chunk),

time: 112 us -> 110 us (0.982)
  Pallas kernels: 111 us -> 109 us
where the time goes in v3:
time: 110 us
  Pallas kernels  109 us (99%)
    pallas_call x1, Pallas kernels, local(): pl.pallas_call(body, out_shape=(jax.ShapeDtypeStruct((piece, d), BF16), w...  105 us
    pallas_call x1, Pallas kernels, local(): pl.pallas_call(hand_over, out_shape=tuple((jax.ShapeDtypeStruct(one.shape...  4.24 us

profile of v3, /device:TPU:1, one launch (start us, length us, event | category | flops | bytes accessed | tf_op | source)
XLA Modules:
  0.0 110.1 jit_solution(14797485552754788575)
XLA Ops:
  0.6 105.1 %shard_map.84 = (bf16[32,1024]{1,0:T(8,128)(2,1)}, bf16[896,1024]{1,0:T(8,128)(2,1)}, bf16[896,1024]{1,0:T(8,128)(2,1)}, bf16[896,1024]{1,0:T(8,128)(2,1)}) custom-call(bf16[32,1024]{1,0:T(8,128)(2,1)} %tok_hbm.1, bf16[896,1024]{1,0:T(8,128)(2,1)} %wg_hbm.1, bf16[896,1024]{1,0:T(8,128)(2,1)} %wu_hbm.1, bf16[896,1024]{1,0:T(8,128)(2,1)} %wd_hbm.1, ...), custom_call_target="tpu_custom_call" | custom-call | flops 15032385536 | bytes 11010048 | tf_op jit(solution)/shard_map/pallas_call | solution.py:577
  105.7 4.2 %shard_map.85 = (bf16[32,1024]{1,0:T(8,128)(2,1)}, bf16[896,1024]{1,0:T(8,128)(2,1)}, bf16[896,1024]{1,0:T(8,128)(2,1)}, bf16[896,1024]{1,0:T(8,128)(2,1)}) custom-call(bf16[32,1024]{1,0:T(8,128)(2,1)} %get-tuple-element.8.refs_0_, bf16[896,1024]{1,0:T(8,128)(2,1)} %get-tuple-element.9.refs_1_, bf16[896,1024]{1,0:T(8,128)(2,1)} %get-tuple-element.10.refs_2_, ...), custom_call_target="tpu_custom_call" | custom-call | bytes 11010048 | tf_op jit(solution)/shard_map/pallas_call | solution.py:590

commit v4 on v3

--- a/solution.py
+++ b/solution.py
@@ -411,99 +411,99 @@
     gather_start()
     gather_near(0, 0)
     gather_far(0, 0)
+    gather_far(0, 1)
+    gather_near(0, 1)
     gate_up_first(0)
     gather_y(1, 0)
     gather_twin(0, 0)
-    gather_far(0, 1)
-    gather_near(0, 1)
+    gather_twin(0, 1)
     gate_up_first(1)
     gather_far(1, 0)
-    gather_y(1, 1)
-    gather_twin(0, 1)
-    gate_up_pass(0)
     gather_y(3, 0)
     gather_z()
+    hid_start(0)
+    gate_up_pass(0)
+    gather_y(1, 1)
     gather_twin(1, 0)
-    hid_start(0)
     gate_up_start(1)
+    gather_far(3, 0)
+    gather_y(2, 0)
+    gate_up_cross(0)
+    hid_cross(0)
+    gather_twin(3, 0)
+    gate_up_pass(1)
     gather_far(1, 1)
-    gather_far(3, 0)
+    hid_start(3)
+    gather_far(2, 0)
+    hid_pass(0)
+    gate_up_start(3)
     gather_twin(1, 1)
-    gather_y(2, 0)
-    gate_up_pass(1)
-    gather_twin(3, 0)
+    gather_twin(2, 0)
     hid_start(1)
-    hid_cross(0)
-    gate_up_start(3)
-    gather_far(2, 0)
+    gate_up_pass(3)
+    hid_cross(3)
+    gate_up_start(2)
+    hid_start(2)
+    hid_pass(3)
+    hid_cross(1)
+    gate_up_pass(2)
+    gate_up_cross(3)
+    hid_cross(2)
     gate_up_cross(1)
-    hid_start(3)
-    gather_twin(2, 0)
-    gate_up_pass(3)
-    hid_cross(1)
-    gate_up_start(2)
     hid_pass(1)
-    hid_start(2)
-    gate_up_pass(2)
+    pointwise(3)
+    gate_up_cross(2)
+    hid_pass(2)
     pointwise(1)
-    gate_up_cross(0)
-    hid_cross(2)
-    gate_up_cross(2)
-    hid_cross(3)
-    gate_up_cross(3)
+    spread_pair(3)
+    pointwise(2)
+    down_start(2)
+    spread_far(3)
+    spread_pair(2)
+    down_start(1)
     spread_pair(1)
-    hid_pass(3)
-    hid_pass(2)
-    down_start(1)
+    input_near(3)
+    input_rows(3)
+    spread_far(2)
+    down_far(1)
+    input_fold(3)
+    down_start(3)
     spread_far(1)
-    pointwise(2)
-    pointwise(3)
-    input_near(1)
-    spread_pair(2)
-    down_start(3)
-    down_far(1)
-    input_rows(1)
-    hid_pass(0)
-    input_fold(1)
-    spread_far(2)
-    spread_pair(3)
     pointwise(0)
+    down_far(2)
     input_near(2)
     input_rows(2)
+    input_fold(2)
+    spread_pair(0)
+    input_pass(3)
+    down_far(3)
+    down_last(1)
+    input_near(1)
+    input_rows(1)
+    input_pass(2)
+    down_start(0)
+    weight_pair(2)
+    input_fold(1)
+    down_last(2)
+    input_own(2)
+    spread_far(0)
+    weight_pair(3)
+    weight_down(1)
     input_pass(1)
-    down_far(3)
-    input_fold(2)
-    down_start(0)
-    spread_far(3)
-    spread_pair(0)
-    weight_pair(2)
-    input_own(1)
-    down_start(2)
-    down_last(1)
-    input_pass(2)
-    weight_pair(1)
-    input_near(3)
-    input_own(2)
     down_last(3)
-    input_rows(3)
-    weight_pair(3)
-    spread_far(0)
     down_far(0)
-    input_fold(3)
-    down_far(2)
     input_near(0)
-    input_pass(3)
     input_rows(0)
     down_last(0)
-    down_last(2)
+    weight_pair(0)
     input_own(3)
+    input_own(1)
     input_far()
     input_fold(0)
-    weight_pair(0)
     weight_down(3)
-    weight_down(1)
+    weight_down(2)
+    weight_pair(1)
     input_pass(0)
-    weight_down(2)
     weight_down(0)
     input_own(0)
     input_out()

time: 110 us -> 109 us (level)
  no operation moved by 1% of the time
where the time goes in v4:
time: 109 us
  Pallas kernels  109 us (100%)
    pallas_call x1, Pallas kernels, local(): pl.pallas_call(body, out_shape=(jax.ShapeDtypeStruct((piece, d), BF16), w...  104 us
    pallas_call x1, Pallas kernels, local(): pl.pallas_call(hand_over, out_shape=tuple((jax.ShapeDtypeStruct(one.shape...  4.24 us

profile of v4, /device:TPU:1, one launch (start us, length us, event | category | flops | bytes accessed | tf_op | source)
XLA Modules:
  0.0 109.3 jit_solution(8150035678231498950)
XLA Ops:
  0.6 104.3 %shard_map.84 = (bf16[32,1024]{1,0:T(8,128)(2,1)}, bf16[896,1024]{1,0:T(8,128)(2,1)}, bf16[896,1024]{1,0:T(8,128)(2,1)}, bf16[896,1024]{1,0:T(8,128)(2,1)}) custom-call(bf16[32,1024]{1,0:T(8,128)(2,1)} %tok_hbm.1, bf16[896,1024]{1,0:T(8,128)(2,1)} %wg_hbm.1, bf16[896,1024]{1,0:T(8,128)(2,1)} %wu_hbm.1, bf16[896,1024]{1,0:T(8,128)(2,1)} %wd_hbm.1, ...), custom_call_target="tpu_custom_call" | custom-call | flops 15032385536 | bytes 11010048 | tf_op jit(solution)/shard_map/pallas_call | solution.py:577
  104.9 4.2 %shard_map.85 = (bf16[32,1024]{1,0:T(8,128)(2,1)}, bf16[896,1024]{1,0:T(8,128)(2,1)}, bf16[896,1024]{1,0:T(8,128)(2,1)}, bf16[896,1024]{1,0:T(8,128)(2,1)}) custom-call(bf16[32,1024]{1,0:T(8,128)(2,1)} %get-tuple-element.8.refs_0_, bf16[896,1024]{1,0:T(8,128)(2,1)} %get-tuple-element.9.refs_1_, bf16[896,1024]{1,0:T(8,128)(2,1)} %get-tuple-element.10.refs_2_, ...), custom_call_target="tpu_custom_call" | custom-call | bytes 11010048 | tf_op jit(solution)/shard_map/pallas_call | solution.py:590

commit v5 on v3

--- a/solution.py
+++ b/solution.py
@@ -411,100 +411,100 @@
     gather_start()
     gather_near(0, 0)
     gather_far(0, 0)
+    gather_far(0, 1)
+    gather_near(0, 1)
     gate_up_first(0)
     gather_y(1, 0)
     gather_twin(0, 0)
-    gather_far(0, 1)
-    gather_near(0, 1)
     gate_up_first(1)
+    gather_z()
+    gather_twin(0, 1)
     gather_far(1, 0)
     gather_y(1, 1)
-    gather_twin(0, 1)
+    hid_start(0)
+    gather_y(3, 0)
     gate_up_pass(0)
-    gather_y(3, 0)
-    gather_z()
     gather_twin(1, 0)
-    hid_start(0)
+    gather_far(1, 1)
     gate_up_start(1)
-    gather_far(1, 1)
     gather_far(3, 0)
     gather_twin(1, 1)
     gather_y(2, 0)
+    hid_cross(0)
+    hid_start(1)
+    gather_twin(3, 0)
     gate_up_pass(1)
-    gather_twin(3, 0)
-    hid_start(1)
-    hid_cross(0)
+    gather_far(2, 0)
+    hid_pass(0)
     gate_up_start(3)
-    gather_far(2, 0)
+    hid_start(3)
     gate_up_cross(1)
-    hid_start(3)
     gather_twin(2, 0)
-    gate_up_pass(3)
     hid_cross(1)
     gate_up_start(2)
+    hid_start(2)
+    gate_up_pass(3)
     hid_pass(1)
-    hid_start(2)
+    gate_up_cross(0)
     gate_up_pass(2)
+    hid_cross(3)
+    hid_cross(2)
     pointwise(1)
-    gate_up_cross(0)
-    hid_cross(2)
+    hid_pass(2)
     gate_up_cross(2)
-    hid_cross(3)
+    spread_pair(1)
     gate_up_cross(3)
-    spread_pair(1)
     hid_pass(3)
-    hid_pass(2)
     down_start(1)
+    pointwise(2)
     spread_far(1)
-    pointwise(2)
+    down_far(1)
+    input_near(1)
     pointwise(3)
-    input_near(1)
+    input_rows(1)
     spread_pair(2)
+    down_last(1)
+    weight_pair(1)
+    input_fold(1)
+    spread_pair(3)
+    spread_far(2)
+    input_pass(1)
     down_start(3)
-    down_far(1)
-    input_rows(1)
-    hid_pass(0)
-    input_fold(1)
-    spread_far(2)
-    spread_pair(3)
+    input_near(2)
+    spread_far(3)
     pointwise(0)
-    input_near(2)
+    input_near(3)
     input_rows(2)
-    input_pass(1)
+    down_start(2)
+    spread_pair(0)
+    input_fold(2)
     down_far(3)
-    input_fold(2)
     down_start(0)
-    spread_far(3)
-    spread_pair(0)
+    input_rows(3)
+    input_own(1)
+    input_pass(2)
     weight_pair(2)
-    input_own(1)
-    down_start(2)
-    down_last(1)
-    input_pass(2)
-    weight_pair(1)
-    input_near(3)
+    input_fold(3)
+    weight_down(1)
+    down_far(2)
+    spread_far(0)
     input_own(2)
+    input_near(0)
+    down_last(2)
     down_last(3)
-    input_rows(3)
+    input_pass(3)
+    down_far(0)
     weight_pair(3)
-    spread_far(0)
-    down_far(0)
-    input_fold(3)
-    down_far(2)
-    input_near(0)
-    input_pass(3)
     input_rows(0)
     down_last(0)
-    down_last(2)
     input_own(3)
+    input_fold(0)
     input_far()
-    input_fold(0)
+    weight_down(3)
     weight_pair(0)
-    weight_down(3)
-    weight_down(1)
     input_pass(0)
+    weight_down(0)
     weight_down(2)
-    weight_down(0)
     input_own(0)
     input_out()
     assert arrived == set(groups)

time: 110 us -> 110 us (level)
  no operation moved by 1% of the time
where the time goes in v5:
time: 110 us
  Pallas kernels  109 us (99%)
    pallas_call x1, Pallas kernels, local(): pl.pallas_call(body, out_shape=(jax.ShapeDtypeStruct((piece, d), BF16), w...  105 us
    pallas_call x1, Pallas kernels, local(): pl.pallas_call(hand_over, out_shape=tuple((jax.ShapeDtypeStruct(one.shape...  4.24 us

profile of v5, /device:TPU:1, one launch (start us, length us, event | category | flops | bytes accessed | tf_op | source)
XLA Modules:
  0.0 109.7 jit_solution(7986530408107670781)
XLA Ops:
  0.6 104.7 %shard_map.84 = (bf16[32,1024]{1,0:T(8,128)(2,1)}, bf16[896,1024]{1,0:T(8,128)(2,1)}, bf16[896,1024]{1,0:T(8,128)(2,1)}, bf16[896,1024]{1,0:T(8,128)(2,1)}) custom-call(bf16[32,1024]{1,0:T(8,128)(2,1)} %tok_hbm.1, bf16[896,1024]{1,0:T(8,128)(2,1)} %wg_hbm.1, bf16[896,1024]{1,0:T(8,128)(2,1)} %wu_hbm.1, bf16[896,1024]{1,0:T(8,128)(2,1)} %wd_hbm.1, ...), custom_call_target="tpu_custom_call" | custom-call | flops 15032385536 | bytes 11010048 | tf_op jit(solution)/shard_map/pallas_call | solution.py:577
  105.3 4.2 %shard_map.85 = (bf16[32,1024]{1,0:T(8,128)(2,1)}, bf16[896,1024]{1,0:T(8,128)(2,1)}, bf16[896,1024]{1,0:T(8,128)(2,1)}, bf16[896,1024]{1,0:T(8,128)(2,1)}) custom-call(bf16[32,1024]{1,0:T(8,128)(2,1)} %get-tuple-element.8.refs_0_, bf16[896,1024]{1,0:T(8,128)(2,1)} %get-tuple-element.9.refs_1_, bf16[896,1024]{1,0:T(8,128)(2,1)} %get-tuple-element.10.refs_2_, ...), custom_call_target="tpu_custom_call" | custom-call | bytes 11010048 | tf_op jit(solution)/shard_map/pallas_call | solution.py:590
